TPU v7x, 32 devices: a whole 2x2x4 slice. The times are simulated.
32 devices in a mesh: band: 4 (over y, core), col: 8 (over z, x).
Axes of the slice: x: 2, y: 2, z: 4, core: 2. Of those that a mesh axis runs over, the one named last changes fastest.
Arguments:
- intersections: bfloat16 [8, 1024, 512], P('band'), may hold values from -6 to 6
- screened: bfloat16 [1024, 1024], P('band', 'col'), may hold values from -0.1875 to 0.1875
- poles: bfloat16 [1024, 1024], P('band', 'col'), may hold values from 0.5 to 4
- gap_energy: float32 [3], replicated, may hold values from 0.3 to 3
- gap_class: int32 [8, 512], P('band'), may hold values from 0 to 2
Outputs:
- sigma: float32 [512, 512], P('band', 'col')
All inputs are finite; a program needn't handle non-finite values.
Results may differ from a plain program's by a relative error of at most 0.0041.
Values may be sent and summed in bfloat16 or wider, within the bound.
A program may use at most 64 MiB of HBM per device.

v0:
```python
import jax
import jax.numpy as jnp
from jax import lax
from jax.sharding import PartitionSpec as P


def make_factors(amp_piece, pole_piece, gap_energy, classes):
    amps = amp_piece.astype(jnp.float32)
    freqs = pole_piece.astype(jnp.float32)
    result = []
    for class_id in range(classes):
        energy = gap_energy[class_id]
        result.append((amps * freqs / (freqs * freqs + energy * energy)).astype(jnp.bfloat16))
    return result


def local(intersections, screened, poles, gap_energy, gap_class):
    bands = intersections.shape[0]
    states = intersections.shape[2]
    columns = screened.shape[1]
    classes = gap_energy.shape[0]
    col_pos = lax.axis_index("col")
    amp_piece = lax.all_gather(screened, "band", axis=0, tiled=True)
    pole_piece = lax.all_gather(poles, "band", axis=0, tiled=True)
    factors = make_factors(amp_piece, pole_piece, gap_energy, classes)
    updated = []
    for add_band_idx in range(bands):
        for add_class_id in range(classes):
            term = lax.dot_general(
                intersections[add_band_idx],
                factors[add_class_id],
                (((0,), (0,)), ((), ())),
                preferred_element_type=jnp.float32,
            )
            updated.append(term)
    sides = tuple(updated)
    partial_value = jnp.zeros((states, states), jnp.float32)
    for band_idx in range(bands):
        side = jnp.zeros((states, columns), jnp.float32)
        for class_id in range(classes):
            picked = (gap_class[band_idx] == class_id).astype(jnp.float32)
            side = side + picked[:, None] * sides[band_idx * classes + class_id]
        right = lax.dynamic_slice_in_dim(intersections[band_idx], col_pos * columns, columns, 0)
        partial_value = partial_value + jnp.dot(
            side.astype(jnp.bfloat16), right, preferred_element_type=jnp.float32
        )
    total_g = columns * lax.axis_size("col")
    total_bands = bands * lax.axis_size("band")
    scale = 1.0 / jnp.sqrt(jnp.float32(total_g * total_bands))
    reduced = lax.psum_scatter(partial_value, "band", scatter_dimension=0, tiled=True)
    block = lax.psum_scatter(reduced, "col", scatter_dimension=1, tiled=True)
    return block * scale


def solution(mesh):
    return jax.shard_map(
        local,
        mesh=mesh,
        in_specs=(P("band", None, None), P("band", "col"), P("band", "col"), P(), P("band", None)),
        out_specs=P("band", "col"),
        check_vma=False,
    )
```

profile of v0, /device:TPU:0, one launch (start us, length us, event | category | flops | bytes accessed | tf_op | source)
XLA Modules:
  0.0 138.1 jit_solution(9072854202075515325)
XLA Ops:
  6.5 0.0 reduce-scatter.5.cloned.1.call-start
  6.5 7.4 %all_gather.6 = bf16[1024,128]{1,0:T(8,128)(2,1)S(1)} all-gather(bf16[256,128]{1,0:T(8,128)(2,1)} %param.6), channel_id=1, replica_groups=mesh['band'=4,'col'=8] {'band'}, dimensions={0}, use_global_device_ids=true | all-gather | bytes 327680 | tf_op jit(solution)/shard_map/all_gather | solution.py:23
  14.0 7.7 %all_gather.7 = bf16[1024,128]{1,0:T(8,128)(2,1)} all-gather(bf16[256,128]{1,0:T(8,128)(2,1)} %param.7), channel_id=1, replica_groups=mesh['band'=4,'col'=8] {'band'}, dimensions={0}, use_global_device_ids=true | all-gather | bytes 327680 | tf_op jit(solution)/shard_map/all_gather | solution.py:24
  21.7 0.8 compare_convert_fusion
  22.5 1.4 fusion.45
  27.6 0.0 copy-start
  27.6 0.0 copy-start.1
  27.6 2.8 %fusion.44 = (bf16[1,1024,512]{2,1,0:T(8,128)(2,1)S(1)}, bf16[1,1024,512]{2,1,0:T(8,128)(2,1)}) fusion(bf16[2,1024,512]{2,1,0:T(8,128)(2,1)} %param.5), kind=kLoop, calls=%fused_computation.50 | loop fusion | bytes 4194304 | tf_op jit(solution)/shard_map/slice | solution.py:30
  30.4 0.0 copy-done
  30.4 0.0 copy-done.1
  30.4 1.1 convolution_multiply_fusion.5
  31.5 1.1 convolution_multiply_fusion.2
  32.6 0.0 copy-start.2
  32.6 0.0 copy-start.5
  32.6 2.1 %fusion.3 = f32[128,512]{1,0:T(8,128)} fusion(f32[128,512]{1,0:T(8,128)} %convolution_multiply_fusion.5, f32[512]{0:T(512)S(1)} %bitcast.38, bf16[2,1024,512]{2,1,0:T(8,128)(2,1)S(1)} %copy-done, bf16[1024,128]{1,0:T(8,128)(2,1)} %all_gather.7, bf16[1024,128]{1,0:T(8,128)(2,1)S(1)} %all_gather.6, f32[]{:T(128)} %bitcast.4), kind=kOutput, calls=%fused_computation.9 | convolution fusion | flops 135266304 | bytes 2099204 | tf_op jit(solution)/shard_map/dot_general | solution.py:29
  34.7 0.0 copy-done.2
  34.7 0.0 copy-done.5
  34.7 1.1 fusion.1
  35.8 0.0 copy-start.3
  35.8 0.0 copy-start.4
  35.8 2.1 %fusion.6 = f32[512,512]{1,0:T(8,128)S(1)} fusion(f32[128,512]{1,0:T(8,128)} %fusion.3, bf16[1,1024,512]{2,1,0:T(8,128)(2,1)} %get-tuple-element.6, s32[]{:T(128)S(6)} %select_n.4, f32[512]{0:T(512)S(1)} %bitcast.36, bf16[1024,128]{1,0:T(8,128)(2,1)} %all_gather.7, bf16[1024,128]{1,0:T(8,128)(2,1)S(1)} %all_gather.6, f32[]{:T(128)} %bitcast.6), kind=kOutput, calls=%fused_computation.13 | convolution fusion | flops 202440704 | bytes 3017220 | tf_op jit(solution)/shard_map/dot_general | solution.py:44
  37.9 0.0 copy-done.3
  37.9 0.0 copy-done.4
  37.9 1.6 %convolution_add_fusion = f32[512,512]{1,0:T(8,128)} fusion(f32[512,512]{1,0:T(8,128)S(1)} %fusion.6, f32[128,512]{1,0:T(8,128)S(1)} %copy-done.4, bf16[1,1024,512]{2,1,0:T(8,128)(2,1)S(1)} %get-tuple-element.5, s32[]{:T(128)S(6)} %select_n.4, f32[512]{0:T(512)S(1)} %bitcast.35, bf16[1024,128]{1,0:T(8,128)(2,1)S(1)} %copy-done.3, ...), kind=kOutput, calls=%fused_computation | convolution fusion | flops 202702848 | bytes 4065288 | tf_op jit(solution)/shard_map/dot_general | solution.py:44
  39.5 0.0 reduce-scatter.5.cloned.1.call-update
  39.5 0.0 reduce-scatter.7.cloned.1.call-start
  39.6 25.3 %reduce-scatter.5.cloned.1.call-done = f32[128,512]{1,0:T(8,128)} async-done(((f32[512,512]{1,0:T(8,128)}), f32[128,512]{1,0:T(8,128)}) %reduce-scatter.5.cloned.1.call-update) | async-done | bytes 262160 | tf_op jit(solution)/shard_map/reduce_scatter | solution.py:50
  64.9 1.8 %copy.9 = f32[128,512]{0,1:T(8,128)} copy(f32[128,512]{1,0:T(8,128)} %reduce-scatter.5.cloned.1.call-done) | data formatting | bytes 524288
  66.7 0.0 reduce-scatter.7.cloned.1.call-update
  66.7 63.1 %reduce-scatter.7.cloned.1.call-done = f32[64,128]{1,0:T(8,128)} async-done(((f32[512,128]{1,0:T(8,128)}), f32[64,128]{1,0:T(8,128)}) %reduce-scatter.7.cloned.1.call-update) | async-done | bytes 32784
  129.9 1.4 bitcast_multiply_fusion
Async XLA Ops:
  6.5 58.4 %reduce-scatter.5.cloned.1.call-start = ((), (), s32[]{:S(2)}) async-start(), calls=%async_computation.2 | async-start | bytes 1310720 | tf_op jit(solution)/shard_map/reduce_scatter | solution.py:50
  27.6 2.8 %copy-start = (bf16[2,1024,512]{2,1,0:T(8,128)(2,1)S(1)}, bf16[2,1024,512]{2,1,0:T(8,128)(2,1)}, u32[]{:S(2)}) copy-start(bf16[2,1024,512]{2,1,0:T(8,128)(2,1)} %param.5) | copy-start | bytes 6291460
  27.6 2.8 %copy-start.1 = (bf16[1024,128]{1,0:T(8,128)(2,1)S(1)}, bf16[1024,128]{1,0:T(8,128)(2,1)}, u32[]{:S(2)}) copy-start(bf16[1024,128]{1,0:T(8,128)(2,1)} %all_gather.7) | copy-start | bytes 786436
  32.6 2.1 %copy-start.2 = (bf16[1024,128]{1,0:T(8,128)(2,1)S(1)}, bf16[1024,128]{1,0:T(8,128)(2,1)}, u32[]{:S(2)}) copy-start(bf16[1024,128]{1,0:T(8,128)(2,1)} %all_gather.7) | copy-start | bytes 786436
  32.6 2.1 %copy-start.5 = (f32[128,512]{1,0:T(8,128)S(1)}, f32[128,512]{1,0:T(8,128)}, u32[]{:S(2)}) copy-start(f32[128,512]{1,0:T(8,128)} %convolution_multiply_fusion.2) | copy-start | bytes 786436
  35.8 2.1 %copy-start.3 = (bf16[1024,128]{1,0:T(8,128)(2,1)S(1)}, bf16[1024,128]{1,0:T(8,128)(2,1)}, u32[]{:S(2)}) copy-start(bf16[1024,128]{1,0:T(8,128)(2,1)} %all_gather.7) | copy-start | bytes 786436
  35.8 2.1 %copy-start.4 = (f32[128,512]{1,0:T(8,128)S(1)}, f32[128,512]{1,0:T(8,128)}, u32[]{:S(2)}) copy-start(f32[128,512]{1,0:T(8,128)} %fusion.1) | copy-start | bytes 786436
  39.5 90.3 %reduce-scatter.7.cloned.1.call-start = ((), (), s32[]{:S(2)}) async-start(), calls=%async_computation.3 | async-start | bytes 294912
Sparse Core Ops, SparseCore 0:
  39.7 25.2 reduce-scatter.4
  68.6 61.2 reduce-scatter.6
where the time goes:
time: 139 us; the launch traced here: 138 us
  waiting for transfers between devices  88.5 us (64%)
  between operations  17.2 us (12%)
  blocking collectives  15.2 us (11%)
  matrix products  9.03 us (6%)
  local copies, waits for them, and re-layouts  5.97 us (4%)
  other arithmetic  2.15 us (2%)
    unnamed x3, waiting for transfers between devices  63.2 us
    reduce_scatter x1, waiting for transfers between devices, local(): lax.psum_scatter(partial_value, 'band', scatter_dimension=0, tiled=True)  25.3 us
    all_gather x1, blocking collectives, local(): pole_piece = lax.all_gather(poles, 'band', axis=0, tiled=True)  7.74 us
    all_gather x1, blocking collectives, local(): amp_piece = lax.all_gather(screened, 'band', axis=0, tiled=True)  7.42 us
    dot_general x4, matrix products, local(): lax.dot_general(intersections[add_band_idx], factors[add_class_id], (((0,...  5.31 us
    dot_general x2, matrix products, local(): jnp.dot(side.astype(jnp.bfloat16), right, preferred_element_type=jnp.floa...  3.72 us
    slice x1, local copies, waits for them, and re-layouts, local(): intersections[add_band_idx]  2.79 us
  transfers between devices with their start and end apart: 2, of which 2 were waited for; matrix products, arithmetic and copies ran while one was open for 0% of the time, Pallas kernels for 0%

commit v1 on v0

v1 whole, which is shorter than its diff:
```python
import functools
import math

import jax
import jax.numpy as jnp
from jax import lax
from jax.experimental import pallas as pl
from jax.experimental.pallas import tpu as pltpu
from jax.sharding import PartitionSpec as P

MESH = pl.DeviceIdType.MESH


def flip(pos, mask):
    bit = 1
    while bit <= mask:
        if mask & bit:
            pos = pos + bit - 2 * bit * lax.rem(lax.div(pos, bit), 2)
        bit *= 2
    return pos


def kernel(
    nband, ncol, classes, scale,
    inter_ref, screened_ref, poles_ref, energy_ref, class_ref, out_ref,
    inter, held, energies, cls, side, side_parts, right_all, right, own,
    core_out, core_in, band_out, band_in, col_out, col_in,
    load_sem, gather_send, gather_recv, core_send, core_recv,
    band_send, band_recv, col_send, col_recv,
):
    me, col = lax.axis_index("band"), lax.axis_index("col")
    bands, _, states = inter.shape
    depth, columns = screened_ref.shape
    half = nband // 2
    width = states // nband
    rows = states // ncol

    barrier = pltpu.get_barrier_semaphore()
    peers = [(flip(me, mask), col) for mask in [1] + list(range(2, nband, 2))]
    peers += [(me, flip(col, piece)) for piece in range(1, ncol)]
    for peer in peers:
        pl.semaphore_signal(barrier, inc=1, device_id=peer, device_id_type=MESH)

    loads = [
        pltpu.make_async_copy(screened_ref, held.at[0, 0], load_sem.at[0]),
        pltpu.make_async_copy(poles_ref, held.at[0, 1], load_sem.at[1]),
        pltpu.make_async_copy(energy_ref, energies, load_sem.at[2]),
        pltpu.make_async_copy(class_ref, cls, load_sem.at[3]),
        pltpu.make_async_copy(inter_ref, inter, load_sem.at[4]),
    ]
    for load in loads:
        load.start()
    pl.semaphore_wait(barrier, len(peers))

    arriving = {}

    def push(slot, bit, part):
        source = (screened_ref, poles_ref)[part] if slot == 0 else held.at[slot, part]
        copy = pltpu.make_async_remote_copy(
            src_ref=source,
            dst_ref=held.at[slot + bit, part],
            send_sem=gather_send.at[slot + bit, part],
            recv_sem=gather_recv.at[slot + bit, part],
            device_id=(flip(me, bit), col),
            device_id_type=MESH,
        )
        copy.start()
        arriving[slot + bit, part] = copy

    bit = half
    while bit:
        push(0, bit, 0)
        push(0, bit, 1)
        bit //= 2
    for load in loads:
        load.wait()

    def add_block(slot):
        amps = held[slot, 0].astype(jnp.float32).T
        freqs = held[slot, 1].astype(jnp.float32).T
        top, square = amps * freqs, freqs * freqs
        factors = []
        for class_id in range(classes):
            energy = energies[class_id]
            factors.append((top / (square + energy * energy)).astype(jnp.bfloat16))
        factors = jnp.concatenate(factors, axis=0)
        start = pl.multiple_of(flip(me, slot) * depth, depth)
        for band in range(bands):
            terms = jnp.dot(
                factors, inter[band, pl.ds(start, depth), :], preferred_element_type=jnp.float32
            )
            picked = jnp.zeros((columns, states), jnp.float32)
            for class_id in range(classes):
                term = terms[class_id * columns:(class_id + 1) * columns]
                picked = jnp.where(cls[band:band + 1, :] == class_id, term, picked)
            place = slice(band * columns, (band + 1) * columns)
            side[place, :] = picked if slot == 0 else side[place, :] + picked

    add_block(0)
    first = pl.multiple_of(col * columns, columns)
    for band in range(bands):
        block = inter[band, pl.ds(first, columns), :].astype(jnp.float32)
        right_all[:, band * columns:(band + 1) * columns] = block.T.astype(jnp.bfloat16)
    for piece in range(ncol):
        start = pl.multiple_of(flip(col, piece) * rows, rows)
        right[piece * rows:(piece + 1) * rows, :] = right_all[pl.ds(start, rows), :]

    for slot in range(1, nband):
        for part in range(2):
            arriving[slot, part].wait_recv()
            bit = (slot & -slot) // 2
            while bit:
                push(slot, bit, part)
                bit //= 2
        add_block(slot)
    for block in range(nband):
        part = side[:, block * width:(block + 1) * width]
        side_parts[block] = part.astype(jnp.bfloat16)

    order = list(range(ncol - 1, -1, -1))

    def sides_of(base):
        return jnp.concatenate(
            [side_parts[flip(base, 2 * k)] for k in range(half)], axis=1
        )

    other = sides_of(flip(me, 1))
    core = {}
    group = max(1, ncol // 2)
    for low in range(ncol - group, -1, -group):
        product = jnp.dot(
            right[low * rows:(low + group) * rows, :], other, preferred_element_type=jnp.float32
        ).astype(jnp.bfloat16)
        for piece in range(low + group - 1, low - 1, -1):
            at = (piece - low) * rows
            for k in range(half):
                core_out[piece, k] = product[at:at + rows, k * width:(k + 1) * width]
            core[piece] = pltpu.make_async_remote_copy(
                src_ref=core_out.at[piece],
                dst_ref=core_in.at[piece],
                send_sem=core_send.at[piece],
                recv_sem=core_recv.at[piece],
                device_id=(flip(me, 1), col),
                device_id_type=MESH,
            )
            core[piece].start()
    own[...] = jnp.dot(right[...], sides_of(me), preferred_element_type=jnp.float32)

    across = {}
    for piece in order:
        core[piece].wait_recv()
        at = slice(piece * rows, (piece + 1) * rows)
        for k in range(half - 1, -1, -1):
            lanes = slice(k * width, (k + 1) * width)
            value = own[at, lanes] + core_in[piece, k].astype(jnp.float32)
            if k == 0:
                own[at, lanes] = value
                continue
            band_out[piece, k] = value.astype(jnp.bfloat16)
            across[piece, k] = pltpu.make_async_remote_copy(
                src_ref=band_out.at[piece, k],
                dst_ref=band_in.at[piece, k],
                send_sem=band_send.at[piece, k],
                recv_sem=band_recv.at[piece, k],
                device_id=(flip(me, 2 * k), col),
                device_id_type=MESH,
            )
            across[piece, k].start()

    last = {}
    for piece in order:
        value = own[piece * rows:(piece + 1) * rows, 0:width]
        for k in range(1, half):
            across[piece, k].wait_recv()
            value = value + band_in[piece, k].astype(jnp.float32)
        if piece == 0:
            break
        col_out[piece] = value.astype(jnp.bfloat16)
        last[piece] = pltpu.make_async_remote_copy(
            src_ref=col_out.at[piece],
            dst_ref=col_in.at[piece],
            send_sem=col_send.at[piece],
            recv_sem=col_recv.at[piece],
            device_id=(me, flip(col, piece)),
            device_id_type=MESH,
        )
        last[piece].start()
    for piece in range(1, ncol):
        last[piece].wait_recv()
        value = value + col_in[piece].astype(jnp.float32)
    out_ref[...] = value * scale

    for group_of in (arriving, core, across, last):
        for copy in group_of.values():
            copy.wait_send()


def local(nband, ncol, intersections, screened, poles, gap_energy, gap_class):
    bands, g_rows, states = intersections.shape
    depth, columns = screened.shape
    classes = gap_energy.shape[0]
    half, width, rows = nband // 2, states // nband, states // ncol
    scale = 1.0 / math.sqrt(columns * ncol * bands * nband)
    bf16, f32 = jnp.bfloat16, jnp.float32
    dma = pltpu.SemaphoreType.DMA
    block = pl.pallas_call(
        functools.partial(kernel, nband, ncol, classes, scale),
        out_shape=jax.ShapeDtypeStruct((rows, width), f32),
        in_specs=[pl.BlockSpec(memory_space=pl.ANY)] * 5,
        out_specs=pl.BlockSpec(memory_space=pltpu.VMEM),
        scratch_shapes=[
            pltpu.VMEM((bands, g_rows, states), bf16),
            pltpu.VMEM((nband, 2, depth, columns), bf16),
            pltpu.SMEM((classes,), f32),
            pltpu.VMEM((bands, states), jnp.int32),
            pltpu.VMEM((bands * columns, states), f32),
            pltpu.VMEM((nband, bands * columns, width), bf16),
            pltpu.VMEM((states, bands * columns), bf16),
            pltpu.VMEM((states, bands * columns), bf16),
            pltpu.VMEM((states, half * width), f32),
            pltpu.VMEM((ncol, half, rows, width), bf16),
            pltpu.VMEM((ncol, half, rows, width), bf16),
            pltpu.VMEM((ncol, half, rows, width), bf16),
            pltpu.VMEM((ncol, half, rows, width), bf16),
            pltpu.VMEM((ncol, rows, width), bf16),
            pltpu.VMEM((ncol, rows, width), bf16),
            dma((5,)),
            dma((nband, 2)), dma((nband, 2)),
            dma((ncol,)), dma((ncol,)),
            dma((ncol, half)), dma((ncol, half)),
            dma((ncol,)), dma((ncol,)),
        ],
        compiler_params=pltpu.CompilerParams(
            collective_id=0, has_side_effects=True, vmem_limit_bytes=56 * 1024 * 1024
        ),
        name="self_energy",
    )(intersections, screened, poles, gap_energy, gap_class)
    return block.T


def solution(mesh):
    return jax.shard_map(
        functools.partial(local, mesh.shape["band"], mesh.shape["col"]),
        mesh=mesh,
        in_specs=(P("band", None, None), P("band", "col"), P("band", "col"), P(), P("band", None)),
        out_specs=P("band", "col"),
        check_vma=False,
    )
```

time: 139 us -> 22.7 us (0.16)
  waiting for transfers between devices: 88.5 us -> 0 us
  Pallas kernels: 0 us -> 21.1 us
  between operations: 17.2 us -> 0.01 us
  blocking collectives: 15.2 us -> 0 us
  matrix products: 9.03 us -> 0 us
  local copies, waits for them, and re-layouts: 5.97 us -> 1.38 us
  other arithmetic: 2.15 us -> 0 us
    unnamed x3 -> x0, waiting for transfers between devices: 63.2 us -> none
    reduce_scatter x1 -> x0, waiting for transfers between devices: 25.3 us -> none  [local(): lax.psum_scatter(partial_value, 'band', scatter_dimension=0, tiled=True)]
    pallas_call x0 -> x1, Pallas kernels: none -> 21.1 us  [local(): pl.pallas_call(functools.partial(kernel, nband, ncol, classes, scale), ou...]
    all_gather x2 -> x0, blocking collectives: 15.2 us -> none  [the longest x1 7.74 us: local(): pole_piece = lax.all_gather(poles, 'band', axis=0, tiled=True)]
    dot_general x6 -> x0, matrix products: 9.03 us -> none  [the longest x4 5.31 us: local(): lax.dot_general(intersections[add_band_idx], factors[add_class_id], (((0,...]
    slice x2 -> x0, local copies, waits for them, and re-layouts: 4.16 us -> none  [the longest x1 2.79 us: local(): intersections[add_band_idx]]
  transfers between devices with their start and end apart: 2 -> 0, of which waited for: 2 -> 0; matrix products, arithmetic and copies ran while one was open for 0% -> 0% of each run, Pallas kernels for 0% -> 0%
where the time goes in v1:
time: 22.7 us; the launch traced here: 22.5 us
  Pallas kernels  21.1 us (93%)
  local copies, waits for them, and re-layouts  1.38 us (6%)
    pallas_call x1, Pallas kernels, local(): pl.pallas_call(functools.partial(kernel, nband, ncol, classes, scale), ou...  21.1 us
    unnamed x1, local copies, waits for them, and re-layouts  1.38 us

profile of v1, /device:TPU:0, one launch (start us, length us, event | category | flops | bytes accessed | tf_op | source)
XLA Modules:
  0.0 22.5 jit_solution(1486577798330456525)
XLA Ops:
  0.0 21.1 %self_energy.1 = f32[64,128]{1,0:T(8,128)} custom-call(bf16[2,1024,512]{2,1,0:T(8,128)(2,1)} %inter_ref.1, bf16[256,128]{1,0:T(8,128)(2,1)} %screened_ref.1, bf16[256,128]{1,0:T(8,128)(2,1)} %poles_ref.1, f32[3]{0:T(128)} %energy_ref.1, s32[2,512]{1,0:T(2,128)} %class_ref.1), custom_call_target="tpu_custom_call" | custom-call | tf_op jit(solution)/shard_map/self_energy/pallas_call | solution.py:206
  21.1 1.4 %copy.7 = f32[128,64]{0,1:T(8,128)} copy(f32[128,64]{0,1:T(8,128)} %bitcast.1) | data formatting | bytes 65536

commit v2 on v1

v2 whole, which is shorter than its diff:
```python
import functools
import math

import jax
import jax.numpy as jnp
from jax import lax
from jax.experimental import pallas as pl
from jax.experimental.pallas import tpu as pltpu
from jax.sharding import PartitionSpec as P

MESH = pl.DeviceIdType.MESH


def flip(pos, mask):
    bit = 1
    while bit <= mask:
        if mask & bit:
            pos = pos + bit - 2 * bit * lax.rem(lax.div(pos, bit), 2)
        bit *= 2
    return pos


def kernel(
    nband, ncol, classes, scale, aligned,
    inter_ref, screened_ref, poles_ref, energy_ref, class_ref, out_ref,
    inter, held, energies, cls, cross, side, side_parts, right_all, right, own,
    band_out, band_in, col_out, col_in,
    load_sem, gather_send, gather_recv, swap_send, swap_recv,
    band_send, band_recv, col_send, col_recv,
):
    me, col = lax.axis_index("band"), lax.axis_index("col")
    bands, _, states = inter_ref.shape
    depth, columns = screened_ref.shape
    half = nband // 2
    width = states // nband
    rows = states // ncol
    sibling = flip(me, 1)
    first = pl.multiple_of(col * columns, columns)

    barrier = pltpu.get_barrier_semaphore()
    peers = [(flip(me, mask), col) for mask in [1] + list(range(2, nband, 2))]
    peers += [(me, flip(col, piece)) for piece in range(1, ncol)]
    for peer in peers:
        pl.semaphore_signal(barrier, inc=1, device_id=peer, device_id_type=MESH)

    def shares(owner, slot):
        out = [(inter_ref.at[:, pl.ds(first, columns), :], cross.at[slot])]
        if not aligned:
            out += [(class_ref, cls.at[slot]), (inter_ref, inter.at[slot])]
            return out
        for k in range(half):
            start = pl.multiple_of(flip(owner, 2 * k) * width, width)
            lanes = slice(k * width, (k + 1) * width)
            out.append((class_ref.at[:, pl.ds(start, width)], cls.at[slot, :, lanes]))
            out.append((inter_ref.at[:, :, pl.ds(start, width)], inter.at[slot, :, :, lanes]))
        return out

    pairs = [
        (screened_ref, held.at[0, 0]), (poles_ref, held.at[0, 1]), (energy_ref, energies),
    ] + shares(me, 0)
    loads = [
        pltpu.make_async_copy(source, target, load_sem.at[n])
        for n, (source, target) in enumerate(pairs)
    ]
    for load in loads:
        load.start()
    pl.semaphore_wait(barrier, len(peers))

    arriving = {}

    def push(slot, bit, part):
        source = (screened_ref, poles_ref)[part] if slot == 0 else held.at[slot, part]
        copy = pltpu.make_async_remote_copy(
            src_ref=source,
            dst_ref=held.at[slot + bit, part],
            send_sem=gather_send.at[slot + bit, part],
            recv_sem=gather_recv.at[slot + bit, part],
            device_id=(flip(me, bit), col),
            device_id_type=MESH,
        )
        copy.start()
        arriving[slot + bit, part] = copy

    bit = half
    while bit:
        push(0, bit, 0)
        push(0, bit, 1)
        bit //= 2
    swap = {}
    for n, (source, target) in enumerate(shares(sibling, 1)):
        swap[n] = pltpu.make_async_remote_copy(
            src_ref=source,
            dst_ref=target,
            send_sem=swap_send.at[n],
            recv_sem=swap_recv.at[n],
            device_id=(sibling, col),
            device_id_type=MESH,
        )
        swap[n].start()
    for load in loads:
        load.wait()

    def add_block(slot):
        amps = held[slot, 0].astype(jnp.float32).T
        freqs = held[slot, 1].astype(jnp.float32).T
        top, square = amps * freqs, freqs * freqs
        factors = []
        for class_id in range(classes):
            energy = energies[class_id]
            factors.append((top / (square + energy * energy)).astype(jnp.bfloat16))
        factors = jnp.concatenate(factors, axis=0)
        start = pl.multiple_of(flip(me, slot) * depth, depth)
        for band in range(2 * bands):
            core, index = divmod(band, bands)
            terms = jnp.dot(
                factors, inter[core, index, pl.ds(start, depth), :],
                preferred_element_type=jnp.float32,
            )
            picked = jnp.zeros((columns, terms.shape[1]), jnp.float32)
            for class_id in range(classes):
                term = terms[class_id * columns:(class_id + 1) * columns]
                picked = jnp.where(cls[core, index:index + 1, :] == class_id, term, picked)
            place = slice(band * columns, (band + 1) * columns)
            side[place, :] = picked if slot == 0 else side[place, :] + picked

    def turn(core):
        for band in range(bands):
            block = cross[core, band].astype(jnp.float32)
            low = (core * bands + band) * columns
            right_all[:, low:low + columns] = block.T.astype(jnp.bfloat16)

    turn(0)
    for copy in swap.values():
        copy.wait_recv()
    add_block(0)
    turn(1)
    for piece in range(ncol):
        start = pl.multiple_of(flip(col, piece) * rows, rows)
        right[piece * rows:(piece + 1) * rows, :] = right_all[pl.ds(start, rows), :]

    for slot in range(1, nband):
        for part in range(2):
            arriving[slot, part].wait_recv()
            bit = (slot & -slot) // 2
            while bit:
                push(slot, bit, part)
                bit //= 2
        add_block(slot)
    if aligned:
        sides = side[...].astype(jnp.bfloat16)
    else:
        for block in range(nband):
            part = side[:, block * width:(block + 1) * width]
            side_parts[block] = part.astype(jnp.bfloat16)
        sides = jnp.concatenate([side_parts[flip(me, 2 * k)] for k in range(half)], axis=1)

    across = {}
    group = max(1, ncol // 2)
    for low in range(ncol - group, -1, -group):
        product = jnp.dot(
            right[low * rows:(low + group) * rows, :], sides, preferred_element_type=jnp.float32
        )
        own[low * rows:(low + group) * rows, :] = product[:, 0:width]
        for piece in range(low + group - 1, low - 1, -1):
            at = slice((piece - low) * rows, (piece - low + 1) * rows)
            for k in range(half - 1, 0, -1):
                band_out[piece, k] = product[at, k * width:(k + 1) * width].astype(jnp.bfloat16)
                across[piece, k] = pltpu.make_async_remote_copy(
                    src_ref=band_out.at[piece, k],
                    dst_ref=band_in.at[piece, k],
                    send_sem=band_send.at[piece, k],
                    recv_sem=band_recv.at[piece, k],
                    device_id=(flip(me, 2 * k), col),
                    device_id_type=MESH,
                )
                across[piece, k].start()

    last = {}
    for piece in range(ncol - 1, -1, -1):
        value = own[piece * rows:(piece + 1) * rows, :]
        for k in range(1, half):
            across[piece, k].wait_recv()
            value = value + band_in[piece, k].astype(jnp.float32)
        if piece == 0:
            break
        col_out[piece] = value.astype(jnp.bfloat16)
        last[piece] = pltpu.make_async_remote_copy(
            src_ref=col_out.at[piece],
            dst_ref=col_in.at[piece],
            send_sem=col_send.at[piece],
            recv_sem=col_recv.at[piece],
            device_id=(me, flip(col, piece)),
            device_id_type=MESH,
        )
        last[piece].start()
    for piece in range(1, ncol):
        last[piece].wait_recv()
        value = value + col_in[piece].astype(jnp.float32)
    out_ref[...] = value * scale

    for group_of in (arriving, swap, across, last):
        for copy in group_of.values():
            copy.wait_send()


def local(nband, ncol, intersections, screened, poles, gap_energy, gap_class):
    bands, g_rows, states = intersections.shape
    depth, columns = screened.shape
    classes = gap_energy.shape[0]
    half, width, rows = nband // 2, states // nband, states // ncol
    scale = 1.0 / math.sqrt(columns * ncol * bands * nband)
    bf16, f32 = jnp.bfloat16, jnp.float32
    dma = pltpu.SemaphoreType.DMA
    aligned = width % 128 == 0
    lanes = half * width if aligned else states
    shares = 1 + 2 * (half if aligned else 1)
    block = pl.pallas_call(
        functools.partial(kernel, nband, ncol, classes, scale, aligned),
        out_shape=jax.ShapeDtypeStruct((rows, width), f32),
        in_specs=[pl.BlockSpec(memory_space=pl.ANY)] * 5,
        out_specs=pl.BlockSpec(memory_space=pltpu.VMEM),
        scratch_shapes=[
            pltpu.VMEM((2, bands, g_rows, lanes), bf16),
            pltpu.VMEM((nband, 2, depth, columns), bf16),
            pltpu.SMEM((classes,), f32),
            pltpu.VMEM((2, bands, lanes), jnp.int32),
            pltpu.VMEM((2, bands, columns, states), bf16),
            pltpu.VMEM((2 * bands * columns, lanes), f32),
            pltpu.VMEM((1 if aligned else nband, 2 * bands * columns, width), bf16),
            pltpu.VMEM((states, 2 * bands * columns), bf16),
            pltpu.VMEM((states, 2 * bands * columns), bf16),
            pltpu.VMEM((states, width), f32),
            pltpu.VMEM((ncol, half, rows, width), bf16),
            pltpu.VMEM((ncol, half, rows, width), bf16),
            pltpu.VMEM((ncol, rows, width), bf16),
            pltpu.VMEM((ncol, rows, width), bf16),
            dma((3 + shares,)),
            dma((nband, 2)), dma((nband, 2)),
            dma((shares,)), dma((shares,)),
            dma((ncol, half)), dma((ncol, half)),
            dma((ncol,)), dma((ncol,)),
        ],
        compiler_params=pltpu.CompilerParams(
            collective_id=0, has_side_effects=True, vmem_limit_bytes=56 * 1024 * 1024
        ),
        name="self_energy",
    )(intersections, screened, poles, gap_energy, gap_class)
    return block.T


def solution(mesh):
    return jax.shard_map(
        functools.partial(local, mesh.shape["band"], mesh.shape["col"]),
        mesh=mesh,
        in_specs=(P("band", None, None), P("band", "col"), P("band", "col"), P(), P("band", None)),
        out_specs=P("band", "col"),
        check_vma=False,
    )
```

time: 22.7 us -> 22.2 us (0.978)
  Pallas kernels: 21.1 us -> 20.7 us
    pallas_call x1, Pallas kernels: 21.1 us -> 20.7 us  [local(): pl.pallas_call(functools.partial(kernel, nband, ncol, classes, scale, ali...]
where the time goes in v2:
time: 22.2 us; the launch traced here: 22.1 us
  Pallas kernels  20.7 us (93%)
  local copies, waits for them, and re-layouts  1.38 us (6%)
    pallas_call x1, Pallas kernels, local(): pl.pallas_call(functools.partial(kernel, nband, ncol, classes, scale, ali...  20.7 us
    unnamed x1, local copies, waits for them, and re-layouts  1.38 us

profile of v2, /device:TPU:0, one launch (start us, length us, event | category | flops | bytes accessed | tf_op | source)
XLA Modules:
  0.0 22.1 jit_solution(11728301605142267980)
XLA Ops:
  0.0 20.7 %self_energy.1 = f32[64,128]{1,0:T(8,128)} custom-call(bf16[2,1024,512]{2,1,0:T(8,128)(2,1)} %inter_ref.1, bf16[256,128]{1,0:T(8,128)(2,1)} %screened_ref.1, bf16[256,128]{1,0:T(8,128)(2,1)} %poles_ref.1, f32[3]{0:T(128)} %energy_ref.1, s32[2,512]{1,0:T(2,128)} %class_ref.1), custom_call_target="tpu_custom_call" | custom-call | tf_op jit(solution)/shard_map/self_energy/pallas_call | solution.py:217
  20.7 1.4 %copy.7 = f32[128,64]{0,1:T(8,128)} copy(f32[128,64]{0,1:T(8,128)} %bitcast.1) | data formatting | bytes 65536

commit v3 on v2

--- a/solution.py
+++ b/solution.py
@@ -23,7 +23,7 @@
 def kernel(
     nband, ncol, classes, scale, aligned,
     inter_ref, screened_ref, poles_ref, energy_ref, class_ref, out_ref,
-    inter, held, energies, cls, cross, side, side_parts, right_all, right, own,
+    inter, held, energies, cls, cross, factors, side, side_parts, right_all, right, own,
     band_out, band_in, col_out, col_in,
     load_sem, gather_send, gather_recv, swap_send, swap_recv,
     band_send, band_recv, col_send, col_recv,
@@ -100,27 +100,28 @@
     for load in loads:
         load.wait()
 
-    def add_block(slot):
+    def make_factors(slot):
         amps = held[slot, 0].astype(jnp.float32).T
         freqs = held[slot, 1].astype(jnp.float32).T
         top, square = amps * freqs, freqs * freqs
-        factors = []
         for class_id in range(classes):
             energy = energies[class_id]
-            factors.append((top / (square + energy * energy)).astype(jnp.bfloat16))
-        factors = jnp.concatenate(factors, axis=0)
+            factor = (top / (square + energy * energy)).astype(jnp.bfloat16)
+            factors[slot, class_id * columns:(class_id + 1) * columns, :] = factor
+
+    def add_block(slot, core):
         start = pl.multiple_of(flip(me, slot) * depth, depth)
-        for band in range(2 * bands):
-            core, index = divmod(band, bands)
+        for index in range(bands):
             terms = jnp.dot(
-                factors, inter[core, index, pl.ds(start, depth), :],
+                factors[slot], inter[core, index, pl.ds(start, depth), :],
                 preferred_element_type=jnp.float32,
             )
             picked = jnp.zeros((columns, terms.shape[1]), jnp.float32)
             for class_id in range(classes):
                 term = terms[class_id * columns:(class_id + 1) * columns]
                 picked = jnp.where(cls[core, index:index + 1, :] == class_id, term, picked)
-            place = slice(band * columns, (band + 1) * columns)
+            low = (core * bands + index) * columns
+            place = slice(low, low + columns)
             side[place, :] = picked if slot == 0 else side[place, :] + picked
 
     def turn(core):
@@ -129,23 +130,33 @@
             low = (core * bands + band) * columns
             right_all[:, low:low + columns] = block.T.astype(jnp.bfloat16)
 
+    make_factors(0)
+    add_block(0, 0)
     turn(0)
-    for copy in swap.values():
-        copy.wait_recv()
-    add_block(0)
-    turn(1)
-    for piece in range(ncol):
-        start = pl.multiple_of(flip(col, piece) * rows, rows)
-        right[piece * rows:(piece + 1) * rows, :] = right_all[pl.ds(start, rows), :]
+
+    def pass_on(slot, part):
+        arriving[slot, part].wait_recv()
+        bit = (slot & -slot) // 2
+        while bit:
+            push(slot, bit, part)
+            bit //= 2
 
     for slot in range(1, nband):
-        for part in range(2):
-            arriving[slot, part].wait_recv()
-            bit = (slot & -slot) // 2
-            while bit:
-                push(slot, bit, part)
-                bit //= 2
-        add_block(slot)
+        pass_on(slot, 0)
+        if slot == half:
+            for copy in swap.values():
+                copy.wait_recv()
+            turn(1)
+            for piece in range(ncol):
+                start = pl.multiple_of(flip(col, piece) * rows, rows)
+                right[piece * rows:(piece + 1) * rows, :] = right_all[pl.ds(start, rows), :]
+            for earlier in range(slot):
+                add_block(earlier, 1)
+        pass_on(slot, 1)
+        make_factors(slot)
+        add_block(slot, 0)
+        if slot >= half:
+            add_block(slot, 1)
     if aligned:
         sides = side[...].astype(jnp.bfloat16)
     else:
@@ -225,6 +236,7 @@
             pltpu.SMEM((classes,), f32),
             pltpu.VMEM((2, bands, lanes), jnp.int32),
             pltpu.VMEM((2, bands, columns, states), bf16),
+            pltpu.VMEM((nband, classes * columns, depth), bf16),
             pltpu.VMEM((2 * bands * columns, lanes), f32),
             pltpu.VMEM((1 if aligned else nband, 2 * bands * columns, width), bf16),
             pltpu.VMEM((states, 2 * bands * columns), bf16),

time: 22.2 us -> 22.1 us (level)
  no operation moved by 1% of the time
where the time goes in v3:
time: 22.1 us; the launch traced here: 21.9 us
  Pallas kernels  20.6 us (93%)
  local copies, waits for them, and re-layouts  1.38 us (6%)
    pallas_call x1, Pallas kernels, local(): pl.pallas_call(functools.partial(kernel, nband, ncol, classes, scale, ali...  20.6 us
    unnamed x1, local copies, waits for them, and re-layouts  1.38 us

profile of v3, /device:TPU:0, one launch (start us, length us, event | category | flops | bytes accessed | tf_op | source)
XLA Modules:
  0.0 21.9 jit_solution(3526363289423517100)
XLA Ops:
  0.0 20.6 %self_energy.1 = f32[64,128]{1,0:T(8,128)} custom-call(bf16[2,1024,512]{2,1,0:T(8,128)(2,1)} %inter_ref.1, bf16[256,128]{1,0:T(8,128)(2,1)} %screened_ref.1, bf16[256,128]{1,0:T(8,128)(2,1)} %poles_ref.1, f32[3]{0:T(128)} %energy_ref.1, s32[2,512]{1,0:T(2,128)} %class_ref.1), custom_call_target="tpu_custom_call" | custom-call | tf_op jit(solution)/shard_map/self_energy/pallas_call | solution.py:228
  20.6 1.4 %copy.7 = f32[128,64]{0,1:T(8,128)} copy(f32[128,64]{0,1:T(8,128)} %bitcast.1) | data formatting | bytes 65536

commit v4 on v3

--- a/solution.py
+++ b/solution.py
@@ -38,7 +38,7 @@
     first = pl.multiple_of(col * columns, columns)
 
     barrier = pltpu.get_barrier_semaphore()
-    peers = [(flip(me, mask), col) for mask in [1] + list(range(2, nband, 2))]
+    peers = [(flip(me, mask), col) for mask in list(range(2, nband, 2)) + [1]]
     peers += [(me, flip(col, piece)) for piece in range(1, ncol)]
     for peer in peers:
         pl.semaphore_signal(barrier, inc=1, device_id=peer, device_id_type=MESH)
@@ -62,8 +62,6 @@
         pltpu.make_async_copy(source, target, load_sem.at[n])
         for n, (source, target) in enumerate(pairs)
     ]
-    for load in loads:
-        load.start()
     pl.semaphore_wait(barrier, len(peers))
 
     arriving = {}
@@ -97,6 +95,8 @@
             device_id_type=MESH,
         )
         swap[n].start()
+    for load in loads:
+        load.start()
     for load in loads:
         load.wait()
 

time: 22.1 us -> 22.1 us (level)
  no operation moved by 1% of the time
where the time goes in v4:
time: 22.1 us; the launch traced here: 21.9 us
  Pallas kernels  20.6 us (93%)
  local copies, waits for them, and re-layouts  1.38 us (6%)
    pallas_call x1, Pallas kernels, local(): pl.pallas_call(functools.partial(kernel, nband, ncol, classes, scale, ali...  20.6 us
    unnamed x1, local copies, waits for them, and re-layouts  1.38 us

profile of v4, /device:TPU:0, one launch (start us, length us, event | category | flops | bytes accessed | tf_op | source)
XLA Modules:
  0.0 21.9 jit_solution(4915050339489686592)
XLA Ops:
  0.0 20.6 %self_energy.1 = f32[64,128]{1,0:T(8,128)} custom-call(bf16[2,1024,512]{2,1,0:T(8,128)(2,1)} %inter_ref.1, bf16[256,128]{1,0:T(8,128)(2,1)} %screened_ref.1, bf16[256,128]{1,0:T(8,128)(2,1)} %poles_ref.1, f32[3]{0:T(128)} %energy_ref.1, s32[2,512]{1,0:T(2,128)} %class_ref.1), custom_call_target="tpu_custom_call" | custom-call | tf_op jit(solution)/shard_map/self_energy/pallas_call | solution.py:228
  20.6 1.4 %copy.7 = f32[128,64]{0,1:T(8,128)} copy(f32[128,64]{0,1:T(8,128)} %bitcast.1) | data formatting | bytes 65536
